TPU v7x, 32 devices: a whole 2x2x4 slice. The times are simulated.
32 devices in a mesh: row: 8 (over z, x), col: 4 (over y, core).
Axes of the slice: x: 2, y: 2, z: 4, core: 2. Of those that a mesh axis runs over, the one named last changes fastest.
Arguments:
- design_levels: int32 [32, 16384], P(None, ('row', 'col')), may hold values from 0 to 16383, each once within a row
- length_scales: float32 [32], replicated, may hold values from 1 to 3
- features: float32 [16384, 256], P(('row', 'col')), may hold values from -0.375 to 0.375
- noise: float32 [16384], P(('row', 'col')), may hold values from 0.25 to 2.5
- panel_index: int32 [1], replicated, may hold values from 0 to 31
Outputs:
- panel_factor: float32 [16384, 512], P('row')
- updated: float32 [16384, 16384], P('row', 'col')
Inputs may be any that keep to these rules, and one draw needn't show every extreme that they name: Each row of design_levels is a permutation of 0 .. 16384 - 1 (a Latin hypercube).
All inputs are finite; a program needn't handle non-finite values.
Results may differ from a plain program's by a relative error of at most 0.0003.
Values sent between devices are 32-bit elements; how exact they have to be, the bound alone decides.
A program may use at most 192 MiB of HBM per device.

v0:
```python
import jax
import jax.numpy as jnp
from jax import lax
from jax.sharding import PartitionSpec as P

N = 16384
PANEL = 512


def from_root(block, axis, holder):
    block = jnp.where(lax.axis_index(axis) == holder, block, jnp.zeros_like(block))
    return lax.psum(block, axis)


def scale_points(levels, scales):
    return (levels.astype(jnp.float32) + 0.5) / N / scales[:, None]


def kernel_block(left_u, right_u, left_h, right_h, left_noise, left_start, right_start):
    left_sq = jnp.sum(left_u * left_u, axis=0)
    right_sq = jnp.sum(right_u * right_u, axis=0)
    cross = lax.dot_general(
        left_u,
        right_u,
        (((0,), (0,)), ((), ())),
        precision=lax.Precision.HIGHEST,
        preferred_element_type=jnp.float32,
    )
    gram = lax.dot_general(
        left_h,
        right_h,
        (((1,), (1,)), ((), ())),
        precision=lax.Precision.HIGHEST,
        preferred_element_type=jnp.float32,
    )
    left_ids = left_start + jnp.arange(left_u.shape[1], dtype=jnp.int32)
    right_ids = right_start + jnp.arange(right_u.shape[1], dtype=jnp.int32)
    same = left_ids[:, None] == right_ids[None, :]
    distance = left_sq[:, None] + right_sq[None, :] - 2.0 * cross
    return (
        jnp.exp(-0.5 * distance) + gram + jnp.where(same, left_noise[:, None], jnp.zeros_like(gram))
    )


def factor_inverse(block):
    lower = jnp.linalg.cholesky(block)
    identity = jnp.eye(block.shape[0], dtype=block.dtype)
    return lax.linalg.triangular_solve(lower, identity, left_side=True, lower=True)


def times_inverse(columns, inverse):
    return jnp.dot(
        columns, inverse.T, precision=lax.Precision.HIGHEST, preferred_element_type=jnp.float32
    )


def shards(design_levels, length_scales, features, noise, panel_index):
    ratio = lax.axis_size("row") // lax.axis_size("col")
    row_pos = lax.axis_index("row")
    col_pos = lax.axis_index("col")
    piece_u = scale_points(design_levels, length_scales)
    row_u, row_h, row_noise = (
        lax.all_gather(piece_u, "col", axis=1, tiled=True),
        lax.all_gather(features, "col", axis=0, tiled=True),
        lax.all_gather(noise, "col", axis=0, tiled=True),
    )
    row_count = row_h.shape[0]
    col_count = row_count * ratio
    parts_u = []
    parts_h = []
    parts_noise = []
    for member in range(ratio):
        got_u, got_h, got_noise = (
            from_root(row_u, "row", col_pos * ratio + member),
            from_root(row_h, "row", col_pos * ratio + member),
            from_root(row_noise, "row", col_pos * ratio + member),
        )
        parts_u.append(got_u)
        parts_h.append(got_h)
        parts_noise.append(got_noise)
    col_u = jnp.concatenate(parts_u, axis=1)
    col_h = jnp.concatenate(parts_h, axis=0)
    row_start = row_pos * row_count
    col_start = col_pos * col_count
    tile = kernel_block(row_u, col_u, row_h, col_h, row_noise, row_start, col_start)
    start = panel_index[0] * PANEL
    owner = start // col_count
    offset = start - owner * col_count
    diag_owner = start // row_count
    diag_offset = start - diag_owner * row_count
    own_columns = lax.dynamic_slice_in_dim(tile, offset, PANEL, 1)
    panel_rows = from_root(own_columns, "col", owner)
    own_block = lax.dynamic_slice_in_dim(panel_rows, diag_offset, PANEL, 0)
    block = from_root(own_block, "row", diag_owner)
    inverse = factor_inverse(block)
    factor_rows = times_inverse(panel_rows, inverse)
    pieces = []
    for member in range(ratio):
        pieces.append(from_root(factor_rows, "row", col_pos * ratio + member))
    factor_cols = jnp.concatenate(pieces, axis=0)
    updated = tile - jnp.dot(
        factor_rows,
        factor_cols.T,
        precision=lax.Precision.HIGHEST,
        preferred_element_type=jnp.float32,
    )
    return (factor_rows, updated)


def solution(mesh):
    in_specs = (P(None, ("row", "col")), P(), P(("row", "col"), None), P(("row", "col")), P())
    out_specs = (P("row", None), P("row", "col"))
    return jax.shard_map(shards, mesh=mesh, in_specs=in_specs, out_specs=out_specs, check_vma=False)
```

profile of v0, /device:TPU:0, one launch (start us, length us, event | category | flops | bytes accessed | tf_op | source)
XLA Modules:
  0.0 1006.0 jit_solution(2579316017768808512)
XLA Ops:
  8.9 7.2 all_gather.9
  17.0 17.9 %all-gather.3.cloned.1.call-done = f32[2048,256]{1,0:T(8,128)} async-done(((f32[512,256]{1,0:T(8,128)}), f32[2048,256]{1,0:T(8,128)}) %all-gather.3.cloned.1.call-update) | async-done | bytes 2097168 | tf_op jit(solution)/shard_map/all_gather | solution.py:64
  39.5 5.2 all-gather
  44.7 165.4 %all-reduce.14.cloned.1.call-done = (f32[32,2048]{1,0:T(8,128)}, f32[32,2048]{1,0:T(8,128)}, f32[2048,256]{1,0:T(8,128)}, f32[2048,256]{1,0:T(8,128)}) async-done(((f32[32,2048]{1,0:T(8,128)}, f32[32,2048]{1,0:T(8,128)}, f32[2048,256]{1,0:T(8,128)}, f32[2048,256]{1,0:T(8,128)}), (f32[32,2048]{1,0:T(8,128)}, f32[32,2048]{1,0:T(8,128)}, f32[2048,256]{1,0:T(8,128)}, ...) | async-done | bytes 4718608 | tf_op jit(solution)/shard_map/psum | solution.py:12
  212.1 30.3 %fusion.50 = f32[2048,4096]{0,1:T(8,128)} fusion(f32[32,2048]{1,0:T(8,128)S(1)} %all_gather.9, f32[32,4096]{1,0:T(8,128)S(1)} %constant_dynamic-update-slice_fusion), kind=kOutput, calls=%fused_computation.103 | convolution fusion | flops 3221225472 | bytes 34340864 | tf_op jit(solution)/shard_map/dot_general | solution.py:22
  242.5 46.6 %fusion = f32[2048,4096]{0,1:T(8,128)} fusion(f32[2048,4096]{0,1:T(8,128)} %fusion.50, f32[2048,256]{1,0:T(8,128)S(1)} %copy-done.1, f32[2048]{0:T(1024)S(1)} %bitcast.59, s32[2048]{0:T(1024)S(1)} %iota_add_fusion.1, f32[4096]{0:T(1024)S(1)} %multiply_reduce_fusion, f32[2048]{0:T(1024)S(1)} %get-tuple-element.42, s32[4096]{0:T(1024)S(1)} %iota_add_fusion, ...), kind=kOutput, calls=%fused_computation.3 | convolution fusion | flops 25837961216 | bytes 73457664 | tf_op jit(solution)/shard_map/dot_general | solution.py:29
  289.1 4.8 dynamic-slice_select_fusion
  294.0 84.4 %all-reduce.8.cloned.1.call-done = f32[2048,512]{0,1:T(8,128)} async-done(((f32[2048,512]{0,1:T(8,128)}), f32[2048,512]{0,1:T(8,128)}) %all-reduce.8.cloned.1.call-update) | async-done | bytes 4194320 | tf_op jit(solution)/shard_map/psum | solution.py:12
  381.7 79.2 %all-reduce.10.cloned.1.call-done = f32[512,512]{0,1:T(8,128)} async-done(((f32[512,512]{0,1:T(8,128)}), f32[512,512]{0,1:T(8,128)}) %all-reduce.10.cloned.1.call-update) | async-done | bytes 1048592 | tf_op jit(solution)/shard_map/psum | solution.py:12
  463.9 11.7 %cholesky.103 = f32[128,128]{1,0:T(8,128)S(1)} custom-call(f32[128,128]{1,0:T(8,128)S(1)} %cholesky.263), custom_call_target="Cholesky" | custom-call | tf_op jit(solution)/shard_map/jit(cholesky)/cholesky | solution.py:46
  476.4 9.8 custom-call.30
  487.0 11.7 %cholesky.215 = f32[128,128]{1,0:T(8,128)S(1)} custom-call(f32[128,128]{1,0:T(8,128)S(1)} %cholesky.267), custom_call_target="Cholesky" | custom-call | tf_op jit(solution)/shard_map/jit(cholesky)/cholesky | solution.py:46
  499.5 10.6 %custom-call.31 = f32[1,128,128]{1,2,0:T(8,128)} custom-call(f32[1,128,128]{2,1,0:T(8,128)S(1)} %get-tuple-element.48), custom_call_target="InvertDiagBlocksLowerTriangular" | custom-call | tf_op jit(solution)/shard_map/jit(cholesky)/cholesky | solution.py:46
  513.6 11.7 %cholesky.236 = f32[128,128]{1,0:T(8,128)S(1)} custom-call(f32[128,128]{1,0:T(8,128)S(1)} %cholesky.272), custom_call_target="Cholesky" | custom-call | tf_op jit(solution)/shard_map/jit(cholesky)/cholesky | solution.py:46
  525.5 9.8 custom-call.32
  536.1 11.9 %cholesky.253 = f32[128,128]{1,0:T(8,128)S(1)} custom-call(f32[128,128]{1,0:T(8,128)S(1)} %convolution_subtract_fusion.6), custom_call_target="Cholesky" | custom-call | tf_op jit(solution)/shard_map/jit(cholesky)/cholesky | solution.py:46
  552.9 10.7 %while.1 = (s32[]{:T(128)}, f32[512,512]{0,1:T(8,128)S(1)}, s32[4,2]{0,1:T(2,128)S(1)}, f32[4,128,128]{2,1,0:T(8,128)}, s32[]{:T(128)}) while((s32[]{:T(128)}, f32[512,512]{0,1:T(8,128)S(1)}, s32[4,2]{0,1:T(2,128)S(1)}, f32[4,128,128]{2,1,0:T(8,128)}, s32[]{:T(128)}) %tuple.35), condition=%wide.while_cond, body=%wide.while_body.sunk | while | flops 2 | bytes 393329 | solution.py:48
  563.6 40.1 %custom-call.33 = f32[4,128,128]{1,2,0:T(8,128)S(1)} custom-call(f32[4,128,128]{2,1,0:T(8,128)} %get-tuple-element.9), custom_call_target="InvertDiagBlocksLowerTriangular" | custom-call | tf_op jit(solution)/shard_map/triangular_solve | solution.py:48
  607.9 15.0 %fusion.7 = f32[2048,512]{1,0:T(8,128)} fusion(f32[2048,512]{0,1:T(8,128)S(1)} %copy-done, f32[128,512]{1,0:T(8,128)S(1)} %fusion.35, f32[128,512]{1,0:T(8,128)S(1)} %fusion.36, f32[128,512]{1,0:T(8,128)S(1)} %fusion.38, f32[128,512]{1,0:T(8,128)S(1)} %fusion.26), kind=kOutput, calls=%fused_computation.23 | convolution fusion | flops 6443237376 | bytes 9437184 | tf_op jit(solution)/shard_map/dot_general | solution.py:52
  622.9 5.6 copy.31
  628.5 6.8 broadcast_select_fusion.1
  635.3 270.9 %all-reduce.12.cloned.1.call-done = (f32[2048,512]{0,1:T(8,128)}, f32[2048,512]{0,1:T(8,128)}) async-done(((f32[2048,512]{0,1:T(8,128)}, f32[2048,512]{0,1:T(8,128)}), (f32[2048,512]{0,1:T(8,128)}, f32[2048,512]{0,1:T(8,128)})) %all-reduce.12.cloned.1.call-update) | async-done | bytes 8388624 | tf_op jit(solution)/shard_map/psum | solution.py:12
  906.2 61.8 %convolution_subtract_fusion = f32[2048,4096]{0,1:T(8,128)} fusion(f32[2048,4096]{0,1:T(8,128)} %fusion, f32[2048,512]{1,0:T(8,128)} %fusion.7, f32[2048,512]{0,1:T(8,128)} %get-tuple-element.30, f32[2048,512]{0,1:T(8,128)} %get-tuple-element.31), kind=kOutput, calls=%fused_computation.4 | convolution fusion | flops 51550093312 | bytes 79691776 | tf_op jit(solution)/shard_map/dot_general | solution.py:101
  967.9 31.1 %copy.34 = f32[2048,4096]{1,0:T(8,128)} copy(f32[2048,4096]{0,1:T(8,128)} %convolution_subtract_fusion) | data formatting | bytes 67108864
  (86 shorter events, 38.7 us)
Async XLA Ops:
  7.2 27.7 %all-gather.3.cloned.1.call-start = ((), (), s32[]{:S(2)}) async-start(), calls=%async_computation | async-start | bytes 2621440 | tf_op jit(solution)/shard_map/all_gather | solution.py:64
  7.9 202.2 %all-reduce.14.cloned.1.call-start = ((), (), s32[]{:S(2)}) async-start(), calls=%async_computation.4 | async-start | bytes 9437184 | tf_op jit(solution)/shard_map/psum | solution.py:12
  17.0 22.6 %copy-start.2 = (f32[512]{0:T(512)S(1)}, f32[512]{0:T(512)}, u32[]{:S(2)}) copy-start(f32[512]{0:T(512)} %param.8) | copy-start | bytes 6148
  38.8 339.6 %all-reduce.8.cloned.1.call-start = ((), (), s32[]{:S(2)}) async-start(), calls=%async_computation.1 | async-start | bytes 8388608 | tf_op jit(solution)/shard_map/psum | solution.py:12
  212.1 30.3 %copy-start.1 = (f32[2048,256]{1,0:T(8,128)S(1)}, f32[2048,256]{1,0:T(8,128)}, u32[]{:S(2)}) copy-start(f32[2048,256]{1,0:T(8,128)} %all-gather.3.cloned.1.call-done) | copy-start | bytes 6291460
  293.9 167.0 %all-reduce.10.cloned.1.call-start = ((), (), s32[]{:S(2)}) async-start(), calls=%async_computation.2 | async-start | bytes 2097152 | tf_op jit(solution)/shard_map/psum | solution.py:12
  380.7 525.4 %all-reduce.12.cloned.1.call-start = ((), (), s32[]{:S(2)}) async-start(), calls=%async_computation.3 | async-start | bytes 16777216 | tf_op jit(solution)/shard_map/psum | solution.py:12
  603.8 4.1 copy-start
Sparse Core Ops, SparseCore 0:
  9.6 25.2 all-gather.2
  39.4 170.6 all-reduce.13
  294.0 84.3 all-reduce.7
  382.8 78.0 all-reduce.9
  635.4 270.6 all-reduce.11
where the time goes:
time: 1010 us
  waiting for transfers between devices  619 us (61%)
  matrix products  161 us (16%)
  other arithmetic  142 us (14%)
  local copies, waits for them, and re-layouts  54.5 us (5%)
  between operations  17.8 us (2%)
  blocking collectives  12.4 us (1%)
    psum x4, waiting for transfers between devices, from_root(): return lax.psum(block, axis)  600 us
    another operation x14, other arithmetic, factor_inverse(): lower = jnp.linalg.cholesky(block)  79.4 us
    dot_general x1, matrix products, shards(): jnp.dot(factor_rows, factor_cols.T, precision=lax.Precision.HIGHEST, pref...  61.8 us
    dot_general x1, matrix products, kernel_block(): lax.dot_general(left_h, right_h, (((1,), (1,)), ((), ())), precision=lax....  46.6 us
    another operation x3, other arithmetic, factor_inverse(): lax.linalg.triangular_solve(lower, identity, left_side=True, lower=True)  40.3 us
    unnamed x8, local copies, waits for them, and re-layouts  32 us
    dot_general x1, matrix products, kernel_block(): lax.dot_general(left_u, right_u, (((0,), (0,)), ((), ())), precision=lax....  30.3 us
  transfers between devices with their start and end apart: 5, of which 5 were waited for; matrix products, arithmetic and copies ran while one was open for 0% of the time, Pallas kernels for 0%

commit v1 on v0

v1 whole, which is shorter than its diff:
```python
import functools
import math

import jax
import jax.numpy as jnp
from jax import lax
from jax.experimental import pallas as pl
from jax.experimental.pallas import tpu as pltpu
from jax.sharding import PartitionSpec as P

BF = jnp.bfloat16
F32 = jnp.float32
LOG2E = math.log2(math.e)
BASE = 128
STRIP = 8
EXT = 40
EK = 256


def split2(x):
    hi = x.astype(BF)
    return hi, (x - hi.astype(F32)).astype(BF)


def split3(x):
    hi = x.astype(BF)
    rest = x - hi.astype(F32)
    mid = rest.astype(BF)
    return hi, mid, (rest - mid.astype(F32)).astype(BF)


def bdot(a, b):
    return jnp.dot(a, b, preferred_element_type=F32)


def dot3(a, b):
    (ah, al), (bh, bl) = a, b
    return bdot(ah, bh) + (bdot(ah, bl) + bdot(al, bh))


def fdot(a, b, dims):
    return lax.dot_general(
        a, b, (dims, ((), ())), precision=lax.Precision.HIGHEST, preferred_element_type=F32
    )


def exponent_operand(ext, inputs, left):
    width = ext.shape[1]
    root = math.sqrt(LOG2E)
    u = ext[:inputs] * root
    h, m, l = [part.astype(F32) for part in split3(u)]
    s = ext[inputs : inputs + 1] * (-0.5 * LOG2E)
    sh, sm, sl = [part.astype(F32) for part in split3(s)]
    row = lax.broadcasted_iota(jnp.int32, (8, width), 0)
    one = jnp.ones((8, width), F32)
    zero = jnp.zeros((8, width), F32)

    def norms(first):
        mine = jnp.where(
            row == first, sh, jnp.where(row == first + 1, sm, jnp.where(row == first + 2, sl, zero))
        )
        other = 3 - first
        ones = jnp.where((row >= other) & (row < other + 3), one, zero)
        return mine + ones

    if left:
        parts = [h, h, m, h, l, m, norms(0)]
    else:
        parts = [h, m, h, l, h, m, norms(3)]
    depth = 6 * inputs + 8
    parts.append(jnp.zeros((EK - depth, width), F32))
    return jnp.concatenate(parts, axis=0)


def factor_diagonal(d):
    n = d.shape[0]
    eye = (
        lax.broadcasted_iota(jnp.int32, (n, n), 0) == lax.broadcasted_iota(jnp.int32, (n, n), 1)
    ).astype(F32)
    rest_a = d
    rest_i = eye
    sub = lax.broadcasted_iota(jnp.int32, (STRIP, 1), 0)
    done = []
    for j in range(n // STRIP):
        strip = jnp.concatenate([rest_a[:STRIP], rest_i[:STRIP]], axis=1)
        first = j * STRIP
        cols = [
            jnp.broadcast_to(strip[:, first + i : first + i + 1], (STRIP, n)) for i in range(STRIP)
        ]
        for i in range(STRIP):
            inv = lax.rsqrt(cols[i][i : i + 1])
            col = cols[i] * inv
            row = strip[i : i + 1] * jnp.concatenate([inv, inv], axis=1)
            below = jnp.where(sub > i, col, 0.0)
            strip = jnp.where(sub == i, row, strip - jnp.concatenate([below, below], axis=1) * row)
            for k in range(i + 1, STRIP):
                cols[k] = cols[k] - below * col[k : k + 1]
        done.append(strip[:, n:])
        if j + 1 < n // STRIP:
            lead = strip[:, :n]
            change = fdot(lead, strip, ((0,), (0,)))[first + STRIP :]
            rest_a = rest_a[STRIP:] - change[:, :n]
            rest_i = rest_i[STRIP:] - change[:, n:]
    return jnp.concatenate(done, axis=0)


def inverse_kernel(inputs, feats, x_ref, hi_ref, lo_ref, t_ref):
    panel = x_ref.shape[1]
    h = x_ref[:feats, :]
    ext = x_ref[feats:, :]
    left = exponent_operand(ext, inputs, True).astype(BF)
    right = exponent_operand(ext, inputs, False).astype(BF)
    e = lax.dot_general(left, right, (((0,), (0,)), ((), ())), preferred_element_type=F32)
    gram = fdot(h, h, ((0,), (0,)))
    rows = lax.broadcasted_iota(jnp.int32, (panel, panel), 0)
    cols = lax.broadcasted_iota(jnp.int32, (panel, panel), 1)
    noise = ext[inputs + 1 : inputs + 2]
    t_ref[...] = jnp.exp2(e) + gram + jnp.where(rows == cols, noise, 0.0)
    count = panel // BASE
    for b in range(count):
        here = pl.ds(b * BASE, BASE)
        w = factor_diagonal(t_ref[here, here])
        r = fdot(w, t_ref[here, :], ((1,), (0,)))
        t_ref[here, :] = r
        t_ref[here, here] = w
        if b + 1 < count:
            below = pl.ds((b + 1) * BASE, panel - (b + 1) * BASE)
            t_ref[below, here] = jnp.zeros((panel - (b + 1) * BASE, BASE), F32)
            t_ref[below, :] = t_ref[below, :] - fdot(
                t_ref[here, below], t_ref[here, :], ((0,), (0,))
            )
    inverse = jnp.where(rows >= cols, t_ref[...], 0.0)
    hi, lo = split2(inverse)
    hi_ref[...] = hi
    lo_ref[...] = lo


def main_kernel(
    inputs,
    feats,
    n_row,
    n_col,
    bm,
    bn,
    where_ref,
    xr_ref,
    xc_ref,
    xp_ref,
    ihi_ref,
    ilo_ref,
    pf_ref,
    out_ref,
    ah,
    al,
    ea,
    bh,
    bl,
    eb,
    pt,
    ptl,
    pe,
    pel,
    ph,
    phl,
    it,
    itl,
    nr,
):
    step = pl.program_id(0)
    panel = xp_ref.shape[1]
    pts = xr_ref.shape[2]
    half = panel // 2
    row_start = where_ref[0]
    col_start = where_ref[1]
    panel_start = where_ref[2]

    @pl.when(step == 0)
    def _():
        hp = xp_ref[:feats, :]
        ext = xp_ref[feats:, :]
        hi, lo = split2(hp)
        ph[...] = hi
        phl[...] = lo
        hi, lo = split2(hp.T)
        pt[...] = hi
        ptl[...] = lo
        pe[...] = exponent_operand(ext, inputs, False).astype(BF)
        pel[...] = exponent_operand(ext, inputs, True).T.astype(BF)
        it[...] = ihi_ref[...].astype(F32).T.astype(BF)
        itl[...] = ilo_ref[...].astype(F32).T.astype(BF)

    @pl.when(step < n_row)
    def _():
        h = split2(xr_ref[0, :feats, :].T)
        ext = xr_ref[0, feats:, :]
        e = exponent_operand(ext, inputs, True).T.astype(BF)
        k = jnp.exp2(bdot(e, pe[...])) + dot3(h, (ph[...], phl[...]))
        first = row_start + step * pts
        rows = first + lax.broadcasted_iota(jnp.int32, (pts, panel), 0)
        cols = panel_start + lax.broadcasted_iota(jnp.int32, (pts, panel), 1)
        noise_col = ext[inputs : inputs + 8].T[:, 1:2]
        k = k + jnp.where(rows == cols, noise_col, 0.0)
        kh, kl = split2(k)
        p0 = dot3(
            (kh[:, :half], kl[:, :half]), (it[:half, :half], itl[:half, :half])
        )
        p1 = dot3((kh, kl), (it[:, half:], itl[:, half:]))
        p = jnp.concatenate([p0, p1], axis=1)
        pf_ref[...] = p
        phi, plo = split2(-p)
        here = pl.ds(pl.multiple_of(step * pts, pts), pts)
        ah[here, :feats] = h[0]
        al[here, :feats] = h[1]
        ah[here, feats:] = phi
        al[here, feats:] = plo
        ea[here, :] = e
        nr[here, :] = jnp.broadcast_to(noise_col, (pts, 128))

    @pl.when((step >= n_row) & (step < n_row + n_col))
    def _():
        at = step - n_row
        h = split2(xc_ref[0, :feats, :])
        ext = xc_ref[0, feats:, :]
        e = exponent_operand(ext, inputs, False).astype(BF)
        k = jnp.exp2(bdot(pel[...], e)) + dot3((pt[...], ptl[...]), h)
        first = col_start + at * pts
        rows = panel_start + lax.broadcasted_iota(jnp.int32, (panel, pts), 0)
        cols = first + lax.broadcasted_iota(jnp.int32, (panel, pts), 1)
        k = k + jnp.where(rows == cols, ext[inputs + 1 : inputs + 2], 0.0)
        kh, kl = split2(k)
        p0 = dot3(
            (ihi_ref[:half, :half], ilo_ref[:half, :half]), (kh[:half], kl[:half])
        )
        p1 = dot3((ihi_ref[half:, :], ilo_ref[half:, :]), (kh, kl))
        phi, plo = split2(jnp.concatenate([p0, p1], axis=0))
        here = pl.ds(pl.multiple_of(at * pts, pts), pts)
        bh[:feats, here] = h[0]
        bl[:feats, here] = h[1]
        bh[feats:, here] = phi
        bl[feats:, here] = plo
        eb[:, here] = e

    @pl.when(step >= n_row + n_col)
    def _():
        at = step - n_row - n_col
        per = eb.shape[1] // bn
        i = at // per
        j = at - i * per
        rs = pl.ds(pl.multiple_of(i * bm, bm), bm)
        cs = pl.ds(pl.multiple_of(j * bn, bn), bn)
        a = (ah[rs, :], al[rs, :])
        b = (bh[:, cs], bl[:, cs])
        out_ref[...] = jnp.exp2(bdot(ea[rs, :], eb[:, cs])) + dot3(a, b)
        r0 = row_start + i * bm
        c0 = col_start + j * bn

        @pl.when((r0 < c0 + bn) & (c0 < r0 + bm))
        def _():
            for q in range(bn // 128):
                rows = r0 + lax.broadcasted_iota(jnp.int32, (bm, 128), 0)
                cols = c0 + q * 128 + lax.broadcasted_iota(jnp.int32, (bm, 128), 1)
                part = pl.ds(q * 128, 128)
                out_ref[:, part] = out_ref[:, part] + jnp.where(rows == cols, nr[rs, :], 0.0)


def shards(n_total, panel, design_levels, length_scales, features, noise, panel_index):
    n_rows = lax.axis_size("row")
    n_cols = lax.axis_size("col")
    ratio = n_rows // n_cols
    row_pos = lax.axis_index("row")
    col_pos = lax.axis_index("col")
    inputs, pts = design_levels.shape
    feats = features.shape[1]
    depth = feats + EXT

    u = (design_levels.astype(F32) + 0.5) / n_total / length_scales[:, None]
    s = jnp.sum(u * u, axis=0, keepdims=True)
    pad = jnp.zeros((EXT - inputs - 2, pts), F32)
    piece = jnp.concatenate([features.T, u, s, noise[None, :], pad], axis=0)

    start = panel_index[0] * panel
    mine = (row_pos * n_cols + col_pos) * pts
    if pts == panel:
        part = jnp.where(mine == start, piece, 0.0)
    else:
        offset = mine - start
        inside = (offset >= 0) & (offset < panel)
        part = lax.dynamic_update_slice(
            jnp.zeros((depth, panel), F32),
            jnp.where(inside, piece, 0.0),
            (0, jnp.where(inside, offset, 0)),
        )
    xp = lax.psum(part, ("row", "col"))

    xr = lax.all_gather(piece, "col", axis=0)
    pairs = []
    for r in range(n_rows):
        for c in range(n_cols):
            to = ((r % ratio) * n_cols + c) * n_cols + r // ratio
            pairs.append((r * n_cols + c, to))
    moved = lax.ppermute(piece, ("row", "col"), pairs)
    xc = lax.all_gather(moved, "row", axis=0)

    ihi, ilo = pl.pallas_call(
        functools.partial(inverse_kernel, inputs, feats),
        out_shape=[jax.ShapeDtypeStruct((panel, panel), BF)] * 2,
        in_specs=[pl.BlockSpec(memory_space=pltpu.VMEM)],
        out_specs=[pl.BlockSpec(memory_space=pltpu.VMEM)] * 2,
        scratch_shapes=[pltpu.VMEM((panel, panel), F32)],
        compiler_params=pltpu.CompilerParams(vmem_limit_bytes=40 * 2**20),
        cost_estimate=pl.CostEstimate(
            flops=60 * 10**9, bytes_accessed=2**21, transcendentals=2**18
        ),
        name="panel_inverse",
    )(xp)

    rows = pts * n_cols
    cols = pts * n_rows
    bm = min(512, rows)
    bn = min(1024, cols)
    per = cols // bn
    tiles = (rows // bm) * per
    lead = n_cols + n_rows
    row_start = row_pos * rows
    col_start = col_pos * cols
    where = jnp.stack([row_start, col_start, start]).astype(jnp.int32)

    def row_map(g, w):
        return (jnp.minimum(g, n_cols - 1), 0, 0)

    def col_map(g, w):
        return (jnp.clip(g - n_cols, 0, n_rows - 1), 0, 0)

    def out_map(g, w):
        t = jnp.maximum(g - lead, 0)
        return (t // per, t % per)

    k_all = feats + panel
    factor_rows, updated = pl.pallas_call(
        functools.partial(main_kernel, inputs, feats, n_cols, n_rows, bm, bn),
        out_shape=[
            jax.ShapeDtypeStruct((rows, panel), F32),
            jax.ShapeDtypeStruct((rows, cols), F32),
        ],
        grid_spec=pltpu.PrefetchScalarGridSpec(
            num_scalar_prefetch=1,
            grid=(lead + tiles,),
            in_specs=[
                pl.BlockSpec((1, depth, pts), row_map),
                pl.BlockSpec((1, depth, pts), col_map),
                pl.BlockSpec((depth, panel), lambda g, w: (0, 0)),
                pl.BlockSpec((panel, panel), lambda g, w: (0, 0)),
                pl.BlockSpec((panel, panel), lambda g, w: (0, 0)),
            ],
            out_specs=[
                pl.BlockSpec((pts, panel), lambda g, w: (jnp.minimum(g, n_cols - 1), 0)),
                pl.BlockSpec((bm, bn), out_map),
            ],
            scratch_shapes=[
                pltpu.VMEM((rows, k_all), BF),
                pltpu.VMEM((rows, k_all), BF),
                pltpu.VMEM((rows, EK), BF),
                pltpu.VMEM((k_all, cols), BF),
                pltpu.VMEM((k_all, cols), BF),
                pltpu.VMEM((EK, cols), BF),
                pltpu.VMEM((panel, feats), BF),
                pltpu.VMEM((panel, feats), BF),
                pltpu.VMEM((EK, panel), BF),
                pltpu.VMEM((panel, EK), BF),
                pltpu.VMEM((feats, panel), BF),
                pltpu.VMEM((feats, panel), BF),
                pltpu.VMEM((panel, panel), BF),
                pltpu.VMEM((panel, panel), BF),
                pltpu.VMEM((rows, 128), F32),
            ],
        ),
        compiler_params=pltpu.CompilerParams(
            dimension_semantics=("arbitrary",), vmem_limit_bytes=56 * 2**20
        ),
        cost_estimate=pl.CostEstimate(
            flops=2 * rows * cols * k_all * 3, bytes_accessed=rows * cols * 4, transcendentals=0
        ),
        name="kernel_update",
    )(where, xr, xc, xp, ihi, ilo)
    return (factor_rows, updated)


def solution(mesh):
    in_specs = (P(None, ("row", "col")), P(), P(("row", "col"), None), P(("row", "col")), P())
    out_specs = (P("row", None), P("row", "col"))

    def run(design_levels, length_scales, features, noise, panel_index):
        body = functools.partial(shards, design_levels.shape[1], 512)
        return jax.shard_map(
            body, mesh=mesh, in_specs=in_specs, out_specs=out_specs, check_vma=False
        )(design_levels, length_scales, features, noise, panel_index)

    return run
```

time: 1010 us -> 320 us (0.32)
  waiting for transfers between devices: 619 us -> 183 us
  matrix products: 161 us -> 0 us
  other arithmetic: 142 us -> 2.59 us
  Pallas kernels: 0 us -> 110 us
  local copies, waits for them, and re-layouts: 54.5 us -> 5.62 us
  blocking collectives: 12.4 us -> 0 us
    psum x4 -> x1, waiting for transfers between devices: 600 us -> 182 us  [shards(): xp = lax.psum(part, ('row', 'col'))]
    dot_general x4 -> x0, matrix products: 154 us -> none  [the longest x1 61.8 us: shards(): jnp.dot(factor_rows, factor_cols.T, precision=lax.Precision.HIGHEST, pref...]
    another operation x17 -> x1, other arithmetic: 120 us -> 0.62 us  [shards(): where = jnp.stack([row_start, col_start, start]).astype(jnp.int32)]
    pallas_call x0 -> x2, Pallas kernels: none -> 110 us  [the longest x1 73.8 us: shards(): pl.pallas_call(functools.partial(main_kernel, inputs, feats, n_cols, n_ro...]
    unnamed x8 -> x11, local copies, waits for them, and re-layouts: 32 us -> 4.79 us
    all_gather x1 -> x2, waiting for transfers between devices: 17.9 us -> 0.01 us  [the longest x1 0.01 us: shards(): xr = lax.all_gather(piece, 'col', axis=0)]
    select_n x4 -> x1, other arithmetic: 17.7 us -> 1.01 us  [shards(): part = jnp.where(mine == start, piece, 0.0)]
    another operation x34 -> x0, local copies, waits for them, and re-layouts: 14.3 us -> none
  transfers between devices with their start and end apart: 5 -> 4, of which waited for: 5 -> 1; matrix products, arithmetic and copies ran while one was open for 0% -> 0% of each run, Pallas kernels for 0% -> 11%
where the time goes in v1:
time: 320 us
  waiting for transfers between devices  183 us (57%)
  Pallas kernels  110 us (34%)
  between operations  16.2 us (5%)
  local copies, waits for them, and re-layouts  5.62 us (2%)
    psum x1, waiting for transfers between devices, shards(): xp = lax.psum(part, ('row', 'col'))  182 us
    pallas_call x1, Pallas kernels, shards(): pl.pallas_call(functools.partial(main_kernel, inputs, feats, n_cols, n_ro...  73.8 us
    pallas_call x1, Pallas kernels, shards(): pl.pallas_call(functools.partial(inverse_kernel, inputs, feats), out_shap...  36.5 us
  transfers between devices with their start and end apart: 4, of which 1 were waited for; matrix products, arithmetic and copies ran while one was open for 0% of the time, Pallas kernels for 11%

profile of v1, /device:TPU:0, one launch (start us, length us, event | category | flops | bytes accessed | tf_op | source)
XLA Modules:
  0.0 319.6 jit_solution(17946758305286594780)
XLA Ops:
  8.0 0.0 all-reduce.2.cloned.1.call-start
  8.7 1.2 copy.7
  10.0 1.0 multiply_reduce_fusion
  10.9 0.8 concatenate.3
  11.7 0.0 copy-start.3
  11.8 1.0 broadcast_select_fusion
  12.8 0.0 all-reduce.2.cloned.1.call-update
  12.8 0.0 all-gather.5.cloned.1.call-start
  12.8 0.0 copy-done.3
  12.9 0.5 all-gather.5.cloned.1.call-update
  13.4 0.0 all-gather.7.cloned.1.call-start
  13.4 1.7 collective-permute-start
  15.2 0.0 collective-permute-done
  15.2 0.0 copy-start.4
  15.2 0.8 copy-done.4
  16.0 0.0 all-gather.7.cloned.1.call-update
  16.0 0.6 pad_add_fusion.where_ref
  16.6 182.5 %all-reduce.2.cloned.1.call-done.x_ref.xp_ref = f32[296,512]{1,0:T(8,128)} async-done(((f32[296,512]{1,0:T(8,128)}), f32[296,512]{1,0:T(8,128)}) %all-reduce.2.cloned.1.call-update) | async-done | bytes 606224 | tf_op jit(solution)/shard_map/psum | solution.py:293
  199.1 1.1 copy-done
  200.2 36.5 %panel_inverse.1 = (bf16[512,512]{1,0:T(8,128)(2,1)S(1)}, bf16[512,512]{1,0:T(8,128)(2,1)S(1)}) custom-call(f32[296,512]{1,0:T(8,128)S(1)} %copy-done), custom_call_target="tpu_custom_call" | custom-call | flops 60000002048 | bytes 2097152 | tf_op jit(solution)/shard_map/panel_inverse/pallas_call | solution.py:304
  236.7 0.0 copy-start.1
  236.7 0.8 copy-done.1
  237.5 0.8 copy-done.2
  238.4 73.8 %kernel_update.1 = (f32[2048,512]{1,0:T(8,128)}, f32[2048,4096]{1,0:T(8,128)}) custom-call(s32[3]{0:T(128)} %pad_add_fusion.where_ref, f32[4,296,512]{2,1,0:T(8,128)} %bitcast.12, f32[8,296,512]{2,1,0:T(8,128)} %bitcast.11, f32[296,512]{1,0:T(8,128)} %all-reduce.2.cloned.1.call-done.x_ref.xp_ref, bf16[512,512]{1,0:T(8,128)(2,1)} %copy-done.1, ...), custom_call_target="tpu_custom_call" | custom-call | flops 38654705664 | bytes 33554432 | tf_op jit(solution)/shard_map/kernel_update/pallas_call | solution.py:339
  (5 shorter events, 0.0 us)
Async XLA Ops:
  8.0 191.1 %all-reduce.2.cloned.1.call-start = ((), (), s32[]{:S(2)}) async-start(), calls=%async_computation | async-start | bytes 1212416 | tf_op jit(solution)/shard_map/psum | solution.py:293
  11.7 1.1 copy-start.3
  12.8 225.6 %all-gather.5.cloned.1.call-start = ((), (), s32[]{:S(2)}) async-start(), calls=%async_computation.1 | async-start | bytes 3031040 | tf_op jit(solution)/shard_map/all_gather | solution.py:295
  13.4 225.0 %all-gather.7.cloned.1.call-start = ((), (), s32[]{:S(2)}) async-start(), calls=%async_computation.2 | async-start | bytes 5455872 | tf_op jit(solution)/shard_map/all_gather | solution.py:302
  13.4 1.7 collective-permute-start
  15.2 0.8 copy-start.4
  199.1 1.1 copy-start
  236.7 0.8 copy-start.1
  237.5 0.8 copy-start.2
Sparse Core Ops, SparseCore 0:
  14.1 184.9 all-reduce.1
Sparse Core Ops, SparseCore 1:
  15.4 34.0 all-gather.4
  52.1 93.8 all-gather.6

commit v2 on v1

--- a/solution.py
+++ b/solution.py
@@ -133,6 +133,70 @@
     hi, lo = split2(inverse)
     hi_ref[...] = hi
     lo_ref[...] = lo
+
+
+def spread_kernel(bits, n_cols, bounds, x_ref, o_ref, buf, send, recv):
+    me = lax.axis_index("row") * n_cols + lax.axis_index("col")
+    partners = []
+    for k in range(bits):
+        bit = lax.rem(lax.div(me, 2**k), 2)
+        other = me + 2**k * (1 - 2 * bit)
+        partners.append((lax.div(other, n_cols), lax.rem(other, n_cols)))
+    barrier = pltpu.get_barrier_semaphore()
+    for device in partners:
+        pl.semaphore_signal(
+            barrier, inc=1, device_id=device, device_id_type=pl.DeviceIdType.MESH
+        )
+    pl.semaphore_wait(barrier, bits)
+    o_ref[...] = x_ref[...]
+
+    def copy(s, q):
+        here = pl.ds(bounds[q], bounds[q + 1] - bounds[q])
+        return pltpu.make_async_remote_copy(
+            src_ref=o_ref.at[here],
+            dst_ref=buf.at[s, here],
+            send_sem=send.at[s, q],
+            recv_sem=recv.at[s, q],
+            device_id=partners[(s + q) % bits],
+            device_id_type=pl.DeviceIdType.MESH,
+        )
+
+    chunks = len(bounds) - 1
+    flying = [copy(0, q) for q in range(chunks)]
+    for one in flying:
+        one.start()
+    for s in range(bits):
+        for q in range(chunks):
+            flying[q].wait()
+            here = pl.ds(bounds[q], bounds[q + 1] - bounds[q])
+            o_ref[here, :] = o_ref[here, :] + buf[s, here, :]
+            if s + 1 < bits:
+                flying[q] = copy(s + 1, q)
+                flying[q].start()
+
+
+def spread(part):
+    n_rows = lax.axis_size("row")
+    n_cols = lax.axis_size("col")
+    bits = (n_rows * n_cols - 1).bit_length()
+    depth, panel = part.shape
+    groups = depth // 8
+    bounds = [8 * (groups * q // bits) for q in range(bits + 1)]
+    return pl.pallas_call(
+        functools.partial(spread_kernel, bits, n_cols, bounds),
+        out_shape=jax.ShapeDtypeStruct(part.shape, F32),
+        in_specs=[pl.BlockSpec(memory_space=pltpu.VMEM)],
+        out_specs=pl.BlockSpec(memory_space=pltpu.VMEM),
+        scratch_shapes=[
+            pltpu.VMEM((bits, depth, panel), F32),
+            pltpu.SemaphoreType.DMA((bits, bits)),
+            pltpu.SemaphoreType.DMA((bits, bits)),
+        ],
+        compiler_params=pltpu.CompilerParams(
+            collective_id=0, has_side_effects=True, vmem_limit_bytes=16 * 2**20
+        ),
+        name="panel_spread",
+    )(part)
 
 
 def main_kernel(
@@ -290,7 +354,7 @@
             jnp.where(inside, piece, 0.0),
             (0, jnp.where(inside, offset, 0)),
         )
-    xp = lax.psum(part, ("row", "col"))
+    xp = spread(part)
 
     xr = lax.all_gather(piece, "col", axis=0)
     pairs = []

time: 320 us -> 241 us (0.75)
  waiting for transfers between devices: 183 us -> 10.3 us
  Pallas kernels: 110 us -> 206 us
    psum x1 -> x0, waiting for transfers between devices: 182 us -> none  [shards(): xp = lax.psum(part, ('row', 'col'))]
    pallas_call x0 -> x1, Pallas kernels: none -> 95.3 us  [spread(): pl.pallas_call(functools.partial(spread_kernel, bits, n_cols, bounds), ou...]
    all_gather x1, waiting for transfers between devices: 0.01 us -> 10.3 us  [shards(): xc = lax.all_gather(moved, 'row', axis=0)]
  transfers between devices with their start and end apart: 4 -> 3, of which waited for: 1 -> 1; matrix products, arithmetic and copies ran while one was open for 0% -> 0% of each run, Pallas kernels for 11% -> 55%
where the time goes in v2:
time: 241 us
  Pallas kernels  206 us (85%)
  between operations  14.8 us (6%)
  waiting for transfers between devices  10.3 us (4%)
  local copies, waits for them, and re-layouts  6.53 us (3%)
    pallas_call x1, Pallas kernels, spread(): pl.pallas_call(functools.partial(spread_kernel, bits, n_cols, bounds), ou...  95.3 us
    pallas_call x1, Pallas kernels, shards(): pl.pallas_call(functools.partial(main_kernel, inputs, feats, n_cols, n_ro...  73.9 us
    pallas_call x1, Pallas kernels, shards(): pl.pallas_call(functools.partial(inverse_kernel, inputs, feats), out_shap...  36.5 us
    all_gather x1, waiting for transfers between devices, shards(): xc = lax.all_gather(moved, 'row', axis=0)  10.3 us
  transfers between devices with their start and end apart: 3, of which 1 were waited for; matrix products, arithmetic and copies ran while one was open for 0% of the time, Pallas kernels for 55%

profile of v2, /device:TPU:0, one launch (start us, length us, event | category | flops | bytes accessed | tf_op | source)
XLA Modules:
  0.0 240.8 jit_solution(12516941612839819221)
XLA Ops:
  7.2 0.0 all-gather.5.cloned.1.call-start
  7.2 1.2 copy.7
  8.5 1.0 multiply_reduce_fusion
  9.4 2.8 %concatenate.3 = f32[296,512]{1,0:T(8,128)} concatenate(f32[256,512]{1,0:T(8,128)S(1)} %bitcast.8, f32[32,512]{1,0:T(8,128)S(1)} %get-tuple-element.7, f32[1,512]{1,0:T(1,128)S(1)} %bitcast.9, f32[1,512]{1,0:T(1,128)} %bitcast.10, f32[6,512]{1,0:T(8,128)S(1)} %broadcast_in_dim.16), dimensions={0} | concatenate | bytes 1212416 | tf_op jit(solution)/shard_map/concatenate | solution.py:343
  12.2 0.0 all-gather.5.cloned.1.call-update
  12.2 0.0 all-gather.7.cloned.1.call-start
  12.3 1.7 collective-permute-start
  14.0 0.0 collective-permute-done
  14.0 0.0 copy-start.3
  14.0 0.8 copy-done.3
  14.8 0.0 all-gather.7.cloned.1.call-update
  15.5 0.1 broadcast_select_fusion.x_ref
  15.6 95.3 %panel_spread.1.x_ref.xp_ref = f32[296,512]{1,0:T(8,128)S(1)} custom-call(f32[296,512]{1,0:T(8,128)S(1)} %broadcast_select_fusion.x_ref), custom_call_target="tpu_custom_call" | custom-call | tf_op jit(solution)/shard_map/panel_spread/pallas_call | solution.py:185
  110.8 0.0 copy-start
  110.9 0.8 pad_add_fusion.where_ref
  111.6 36.5 %panel_inverse.1 = (bf16[512,512]{1,0:T(8,128)(2,1)S(1)}, bf16[512,512]{1,0:T(8,128)(2,1)S(1)}) custom-call(f32[296,512]{1,0:T(8,128)S(1)} %panel_spread.1.x_ref.xp_ref), custom_call_target="tpu_custom_call" | custom-call | flops 60000002048 | bytes 2097152 | tf_op jit(solution)/shard_map/panel_inverse/pallas_call | solution.py:368
  148.1 0.0 copy-done
  148.1 0.0 copy-start.1
  148.2 0.8 copy-done.1
  149.0 0.0 copy-start.2
  149.0 0.8 copy-done.2
  149.8 0.0 all-gather.5.cloned.1.call-done
  149.8 10.3 %all-gather.7.cloned.1.call-done = f32[2368,512]{1,0:T(8,128)} async-done(((f32[296,512]{1,0:T(8,128)}), f32[2368,512]{1,0:T(8,128)}) %all-gather.7.cloned.1.call-update) | async-done | bytes 4849680 | tf_op jit(solution)/shard_map/all_gather | solution.py:366
  160.1 73.9 %kernel_update.1 = (f32[2048,512]{1,0:T(8,128)}, f32[2048,4096]{1,0:T(8,128)}) custom-call(s32[3]{0:T(128)} %pad_add_fusion.where_ref, f32[4,296,512]{2,1,0:T(8,128)} %bitcast.12, f32[8,296,512]{2,1,0:T(8,128)} %bitcast.11, f32[296,512]{1,0:T(8,128)} %copy-done, bf16[512,512]{1,0:T(8,128)(2,1)} %copy-done.1, bf16[512,512]{1,0:T(8,128)(2,1)} %copy-done.2), custom_call_target="tpu_custom_call" | custom-call | flops 38654705664 | bytes 33554432 | tf_op jit(solution)/shard_map/kernel_update/pallas_call | solution.py:403
  (1 shorter events, 0.0 us)
Async XLA Ops:
  7.2 142.7 %all-gather.5.cloned.1.call-start = ((), (), s32[]{:S(2)}) async-start(), calls=%async_computation | async-start | bytes 3031040 | tf_op jit(solution)/shard_map/all_gather | solution.py:359
  12.2 147.9 %all-gather.7.cloned.1.call-start = ((), (), s32[]{:S(2)}) async-start(), calls=%async_computation.1 | async-start | bytes 5455872 | tf_op jit(solution)/shard_map/all_gather | solution.py:366
  12.3 1.7 collective-permute-start
  14.0 0.8 copy-start.3
  110.8 37.3 %copy-start = (f32[296,512]{1,0:T(8,128)}, f32[296,512]{1,0:T(8,128)S(1)}, u32[]{:S(2)}) copy-start(f32[296,512]{1,0:T(8,128)S(1)} %panel_spread.1.x_ref.xp_ref) | copy-start | bytes 1818628
  148.1 0.9 copy-start.1
  149.0 0.8 copy-start.2
Sparse Core Ops, SparseCore 0:
  12.4 34.9 all-gather.4
  50.1 109.9 all-gather.6

commit v3 on v2

--- a/solution.py
+++ b/solution.py
@@ -135,8 +135,9 @@
     lo_ref[...] = lo
 
 
-def spread_kernel(bits, n_cols, bounds, x_ref, o_ref, buf, send, recv):
-    me = lax.axis_index("row") * n_cols + lax.axis_index("col")
+def spread_kernel(bits, n_cols, bounds, x_ref, mine_ref, o_ref, all_ref, buf, send, recv, send_all, recv_all):
+    col = lax.axis_index("col")
+    me = lax.axis_index("row") * n_cols + col
     partners = []
     for k in range(bits):
         bit = lax.rem(lax.div(me, 2**k), 2)
@@ -149,6 +150,23 @@
         )
     pl.semaphore_wait(barrier, bits)
     o_ref[...] = x_ref[...]
+    all_ref[col] = mine_ref[...]
+    col_bits = (n_cols - 1).bit_length()
+
+    def row_copies(s):
+        k = col_bits - 1 - s
+        low = lax.rem(col, 2 ** (k + 1))
+        return [
+            pltpu.make_async_remote_copy(
+                src_ref=all_ref.at[low + 2 ** (k + 1) * upper],
+                dst_ref=all_ref.at[low + 2 ** (k + 1) * upper],
+                send_sem=send_all.at[s, upper],
+                recv_sem=recv_all.at[s, upper],
+                device_id=partners[k],
+                device_id_type=pl.DeviceIdType.MESH,
+            )
+            for upper in range(2**s)
+        ]
 
     def copy(s, q):
         here = pl.ds(bounds[q], bounds[q + 1] - bounds[q])
@@ -165,6 +183,9 @@
     flying = [copy(0, q) for q in range(chunks)]
     for one in flying:
         one.start()
+    row_flying = row_copies(0)
+    for one in row_flying:
+        one.start()
     for s in range(bits):
         for q in range(chunks):
             flying[q].wait()
@@ -173,9 +194,18 @@
             if s + 1 < bits:
                 flying[q] = copy(s + 1, q)
                 flying[q].start()
-
-
-def spread(part):
+        stage = s - (bits - 1 - col_bits)
+        if stage >= 0:
+            for one in row_flying:
+                one.wait()
+            row_flying = []
+            if stage + 1 < col_bits:
+                row_flying = row_copies(stage + 1)
+                for one in row_flying:
+                    one.start()
+
+
+def spread(part, piece):
     n_rows = lax.axis_size("row")
     n_cols = lax.axis_size("col")
     bits = (n_rows * n_cols - 1).bit_length()
@@ -184,19 +214,24 @@
     bounds = [8 * (groups * q // bits) for q in range(bits + 1)]
     return pl.pallas_call(
         functools.partial(spread_kernel, bits, n_cols, bounds),
-        out_shape=jax.ShapeDtypeStruct(part.shape, F32),
-        in_specs=[pl.BlockSpec(memory_space=pltpu.VMEM)],
-        out_specs=pl.BlockSpec(memory_space=pltpu.VMEM),
+        out_shape=[
+            jax.ShapeDtypeStruct(part.shape, F32),
+            jax.ShapeDtypeStruct((n_cols,) + piece.shape, F32),
+        ],
+        in_specs=[pl.BlockSpec(memory_space=pltpu.VMEM)] * 2,
+        out_specs=[pl.BlockSpec(memory_space=pltpu.VMEM)] * 2,
         scratch_shapes=[
             pltpu.VMEM((bits, depth, panel), F32),
             pltpu.SemaphoreType.DMA((bits, bits)),
             pltpu.SemaphoreType.DMA((bits, bits)),
+            pltpu.SemaphoreType.DMA((bits, n_cols)),
+            pltpu.SemaphoreType.DMA((bits, n_cols)),
         ],
         compiler_params=pltpu.CompilerParams(
             collective_id=0, has_side_effects=True, vmem_limit_bytes=16 * 2**20
         ),
         name="panel_spread",
-    )(part)
+    )(part, piece)
 
 
 def main_kernel(
@@ -354,9 +389,8 @@
             jnp.where(inside, piece, 0.0),
             (0, jnp.where(inside, offset, 0)),
         )
-    xp = spread(part)
-
-    xr = lax.all_gather(piece, "col", axis=0)
+    xp, xr = spread(part, piece)
+
     pairs = []
     for r in range(n_rows):
         for c in range(n_cols):

time: 241 us -> 239 us (level)
  waiting for transfers between devices: 10.3 us -> 5.64 us
  Pallas kernels: 206 us -> 210 us
    all_gather x1, waiting for transfers between devices: 10.3 us -> 5.62 us  [shards(): xc = lax.all_gather(moved, 'row', axis=0)]
    pallas_call x1, Pallas kernels: 95.3 us -> 99.4 us  [spread(): pl.pallas_call(functools.partial(spread_kernel, bits, n_cols, bounds), ou...]
    unnamed x9 -> x11, local copies, waits for them, and re-layouts: 3.72 us -> 5.21 us
  transfers between devices with their start and end apart: 3 -> 2, of which waited for: 1 -> 1; matrix products, arithmetic and copies ran while one was open for 0% -> 0% of each run, Pallas kernels for 55% -> 57%
where the time goes in v3:
time: 239 us
  Pallas kernels  210 us (88%)
  between operations  14.8 us (6%)
  local copies, waits for them, and re-layouts  6.04 us (3%)
  waiting for transfers between devices  5.64 us (2%)
    pallas_call x1, Pallas kernels, spread(): pl.pallas_call(functools.partial(spread_kernel, bits, n_cols, bounds), ou...  99.4 us
    pallas_call x1, Pallas kernels, shards(): pl.pallas_call(functools.partial(main_kernel, inputs, feats, n_cols, n_ro...  73.8 us
    pallas_call x1, Pallas kernels, shards(): pl.pallas_call(functools.partial(inverse_kernel, inputs, feats), out_shap...  36.5 us
    all_gather x1, waiting for transfers between devices, shards(): xc = lax.all_gather(moved, 'row', axis=0)  5.62 us
    unnamed x11, local copies, waits for them, and re-layouts  5.21 us
  transfers between devices with their start and end apart: 2, of which 1 were waited for; matrix products, arithmetic and copies ran while one was open for 0% of the time, Pallas kernels for 57%

profile of v3, /device:TPU:0, one launch (start us, length us, event | category | flops | bytes accessed | tf_op | source)
XLA Modules:
  0.0 238.6 jit_solution(5445141444998966458)
XLA Ops:
  7.2 0.0 all-gather.3.cloned.1.call-start
  7.2 1.2 copy.7
  8.5 1.0 multiply_reduce_fusion
  9.4 0.8 concatenate.3.mine_ref
  10.2 0.7 collective-permute-start
  11.0 0.0 collective-permute-done
  11.0 0.0 copy-start.4
  11.0 0.8 copy-done.4
  11.8 0.0 all-gather.3.cloned.1.call-update
  12.5 99.4 %panel_spread.1 = (f32[296,512]{1,0:T(8,128)S(1)}, f32[4,296,512]{2,1,0:T(8,128)S(1)}) custom-call(f32[296,512]{1,0:T(8,128)S(1)} %broadcast_select_fusion.x_ref, f32[296,512]{1,0:T(8,128)S(1)} %concatenate.3.mine_ref), custom_call_target="tpu_custom_call" | custom-call | tf_op jit(solution)/shard_map/panel_spread/pallas_call | solution.py:215
  111.9 0.0 copy-start
  111.9 1.5 copy-done
  113.4 0.0 copy-start.1
  113.4 0.7 pad_add_fusion.where_ref
  114.1 36.5 %panel_inverse.1 = (bf16[512,512]{1,0:T(8,128)(2,1)S(1)}, bf16[512,512]{1,0:T(8,128)(2,1)S(1)}) custom-call(f32[296,512]{1,0:T(8,128)S(1)} %get-tuple-element.7.x_ref.xp_ref), custom_call_target="tpu_custom_call" | custom-call | flops 60000002048 | bytes 2097152 | tf_op jit(solution)/shard_map/panel_inverse/pallas_call | solution.py:402
  150.6 0.0 copy-done.1
  150.6 0.0 copy-start.2
  150.6 0.8 copy-done.2
  151.4 0.0 copy-start.3
  151.4 0.8 copy-done.3
  152.3 5.6 %all-gather.3.cloned.1.call-done = f32[2368,512]{1,0:T(8,128)} async-done(((f32[296,512]{1,0:T(8,128)}), f32[2368,512]{1,0:T(8,128)}) %all-gather.3.cloned.1.call-update) | async-done | bytes 4849680 | tf_op jit(solution)/shard_map/all_gather | solution.py:400
  157.9 73.8 %kernel_update.1 = (f32[2048,512]{1,0:T(8,128)}, f32[2048,4096]{1,0:T(8,128)}) custom-call(s32[3]{0:T(128)} %pad_add_fusion.where_ref, f32[4,296,512]{2,1,0:T(8,128)} %copy-done, f32[8,296,512]{2,1,0:T(8,128)} %bitcast.10, f32[296,512]{1,0:T(8,128)} %copy-done.1, bf16[512,512]{1,0:T(8,128)(2,1)} %copy-done.2, bf16[512,512]{1,0:T(8,128)(2,1)} %copy-done.3), custom_call_target="tpu_custom_call" | custom-call | flops 38654705664 | bytes 33554432 | tf_op jit(solution)/shard_map/kernel_update/pallas_call | solution.py:437
  (2 shorter events, 0.0 us)
Async XLA Ops:
  7.2 150.7 %all-gather.3.cloned.1.call-start = ((), (), s32[]{:S(2)}) async-start(), calls=%async_computation | async-start | bytes 5455872 | tf_op jit(solution)/shard_map/all_gather | solution.py:400
  10.2 0.7 collective-permute-start
  11.0 0.8 copy-start.4
  111.9 1.5 copy-start
  113.4 37.2 %copy-start.1 = (f32[296,512]{1,0:T(8,128)}, f32[296,512]{1,0:T(8,128)S(1)}, u32[]{:S(2)}) copy-start(f32[296,512]{1,0:T(8,128)S(1)} %get-tuple-element.7.x_ref.xp_ref) | copy-start | bytes 1818628
  150.6 0.9 copy-start.2
  151.4 0.8 copy-start.3
Sparse Core Ops, SparseCore 0:
  11.9 145.9 all-gather.2

commit v4 on v3

--- a/solution.py
+++ b/solution.py
@@ -229,6 +229,9 @@
         ],
         compiler_params=pltpu.CompilerParams(
             collective_id=0, has_side_effects=True, vmem_limit_bytes=16 * 2**20
+        ),
+        cost_estimate=pl.CostEstimate(
+            flops=60 * 10**9, bytes_accessed=2**22, transcendentals=0
         ),
         name="panel_spread",
     )(part, piece)
@@ -397,6 +400,7 @@
             to = ((r % ratio) * n_cols + c) * n_cols + r // ratio
             pairs.append((r * n_cols + c, to))
     moved = lax.ppermute(piece, ("row", "col"), pairs)
+    moved, xp = lax.optimization_barrier((moved, xp))
     xc = lax.all_gather(moved, "row", axis=0)
 
     ihi, ilo = pl.pallas_call(

time: 239 us -> 256 us (1.071)
  waiting for transfers between devices: 5.64 us -> 45 us
  Pallas kernels: 210 us -> 187 us
    all_gather x1, waiting for transfers between devices: 5.62 us -> 45 us  [shards(): xc = lax.all_gather(moved, 'row', axis=0)]
    pallas_call x1, Pallas kernels: 99.4 us -> 77.1 us  [spread(): pl.pallas_call(functools.partial(spread_kernel, bits, n_cols, bounds), ou...]
  transfers between devices with their start and end apart: 2 -> 2, of which waited for: 1 -> 1; matrix products, arithmetic and copies ran while one was open for 0% -> 0% of each run, Pallas kernels for 57% -> 44%
where the time goes in v4:
time: 256 us
  Pallas kernels  187 us (73%)
  waiting for transfers between devices  45 us (18%)
  between operations  14.8 us (6%)
  local copies, waits for them, and re-layouts  6.08 us (2%)
    pallas_call x1, Pallas kernels, spread(): pl.pallas_call(functools.partial(spread_kernel, bits, n_cols, bounds), ou...  77.1 us
    pallas_call x1, Pallas kernels, shards(): pl.pallas_call(functools.partial(main_kernel, inputs, feats, n_cols, n_ro...  73.9 us
    all_gather x1, waiting for transfers between devices, shards(): xc = lax.all_gather(moved, 'row', axis=0)  45 us
    pallas_call x1, Pallas kernels, shards(): pl.pallas_call(functools.partial(inverse_kernel, inputs, feats), out_shap...  36.5 us
    unnamed x11, local copies, waits for them, and re-layouts  5.24 us
  transfers between devices with their start and end apart: 2, of which 1 were waited for; matrix products, arithmetic and copies ran while one was open for 0% of the time, Pallas kernels for 44%

profile of v4, /device:TPU:0, one launch (start us, length us, event | category | flops | bytes accessed | tf_op | source)
XLA Modules:
  0.0 255.7 jit_solution(17683018622914364920)
XLA Ops:
  7.2 0.0 all-gather.3.cloned.1.call-start
  7.2 1.2 copy.7
  8.5 1.0 multiply_reduce_fusion
  9.4 0.8 concatenate.3.mine_ref
  10.2 0.7 collective-permute-start
  11.7 77.1 %panel_spread.1 = (f32[296,512]{1,0:T(8,128)S(1)}, f32[4,296,512]{2,1,0:T(8,128)S(1)}) custom-call(f32[296,512]{1,0:T(8,128)S(1)} %broadcast_select_fusion.x_ref, f32[296,512]{1,0:T(8,128)S(1)} %concatenate.3.mine_ref), custom_call_target="tpu_custom_call" | custom-call | flops 60000002048 | bytes 4194304 | tf_op jit(solution)/shard_map/panel_spread/pallas_call | solution.py:215
  88.8 0.0 copy-start
  88.8 1.5 copy-done
  90.3 0.0 copy-start.1
  90.3 0.0 collective-permute-done
  90.3 0.0 copy-start.4
  90.3 0.8 copy-done.4
  91.1 0.0 all-gather.3.cloned.1.call-update
  91.2 0.7 pad_add_fusion.where_ref
  91.8 36.5 %panel_inverse.1 = (bf16[512,512]{1,0:T(8,128)(2,1)S(1)}, bf16[512,512]{1,0:T(8,128)(2,1)S(1)}) custom-call(f32[296,512]{1,0:T(8,128)S(1)} %get-tuple-element.11.x_ref.xp_ref), custom_call_target="tpu_custom_call" | custom-call | flops 60000002048 | bytes 2097152 | tf_op jit(solution)/shard_map/panel_inverse/pallas_call | solution.py:406
  128.3 0.0 copy-done.1
  128.3 0.0 copy-start.2
  128.3 0.8 copy-done.2
  129.2 0.0 copy-start.3
  129.2 0.8 copy-done.3
  130.0 45.0 %all-gather.3.cloned.1.call-done = f32[2368,512]{1,0:T(8,128)} async-done(((f32[296,512]{1,0:T(8,128)}), f32[2368,512]{1,0:T(8,128)}) %all-gather.3.cloned.1.call-update) | async-done | bytes 4849680 | tf_op jit(solution)/shard_map/all_gather | solution.py:404
  175.0 73.9 %kernel_update.1 = (f32[2048,512]{1,0:T(8,128)}, f32[2048,4096]{1,0:T(8,128)}) custom-call(s32[3]{0:T(128)} %pad_add_fusion.where_ref, f32[4,296,512]{2,1,0:T(8,128)} %copy-done, f32[8,296,512]{2,1,0:T(8,128)} %bitcast.10, f32[296,512]{1,0:T(8,128)} %copy-done.1, bf16[512,512]{1,0:T(8,128)(2,1)} %copy-done.2, bf16[512,512]{1,0:T(8,128)(2,1)} %copy-done.3), custom_call_target="tpu_custom_call" | custom-call | flops 38654705664 | bytes 33554432 | tf_op jit(solution)/shard_map/kernel_update/pallas_call | solution.py:441
  (2 shorter events, 0.0 us)
Async XLA Ops:
  7.2 167.9 %all-gather.3.cloned.1.call-start = ((), (), s32[]{:S(2)}) async-start(), calls=%async_computation | async-start | bytes 5455872 | tf_op jit(solution)/shard_map/all_gather | solution.py:404
  10.2 80.0 %collective-permute-start = (f32[296,512]{1,0:T(8,128)S(1)}, f32[296,512]{1,0:T(8,128)S(1)}, u32[]{:S(2)}, u32[]{:S(2)}) collective-permute-start(f32[296,512]{1,0:T(8,128)S(1)} %concatenate.3.mine_ref), channel_id=1, source_target_pairs={{0,0},{1,4},{2,8},{3,12},{4,16},{5,20},{6,24},{7,28},{8,1},{9,5},{... | collective-permute-start | bytes 1818632 | tf_op jit(solution)/shard_map/ppermute | solution.py:402
  88.8 1.5 copy-start
  90.3 38.0 %copy-start.1 = (f32[296,512]{1,0:T(8,128)}, f32[296,512]{1,0:T(8,128)S(1)}, u32[]{:S(2)}) copy-start(f32[296,512]{1,0:T(8,128)S(1)} %get-tuple-element.11.x_ref.xp_ref) | copy-start | bytes 1818628
  90.3 0.9 copy-start.4
  128.3 0.9 copy-start.2
  129.2 0.8 copy-start.3
Sparse Core Ops, SparseCore 0:
  91.3 83.6 all-gather.2
